TPU v7x, 32 devices: a whole 2x2x4 slice. The times are simulated.
32 devices in a mesh: dp: 8 (over z, y), mp: 4 (over x, core).
Axes of the slice: x: 2, y: 2, z: 4, core: 2. Of those that a mesh axis runs over, the one named last changes fastest.
Arguments:
- inputs: bfloat16 [16384, 1024], P(('dp', 'mp')), may hold values from -6 to 6
- in_proj: bfloat16 [3, 1024, 1024], P(None, None, 'mp'), may hold values from -0.1875 to 0.1875
- qv_bias: float32 [2, 1024], P(None, 'mp'), may hold values from -3 to 3
- out_proj: bfloat16 [1024, 1024], P('mp'), may hold values from -0.5 to 0.5
- out_bias: float32 [1024], replicated, may hold values from -3 to 3
- attn_gain: float32 [1024], replicated, may hold values from 0.25 to 1.75
- attn_shift: float32 [1024], replicated, may hold values from -3 to 3
- up_proj: bfloat16 [1024, 4096], P(None, 'mp'), may hold values from -0.1875 to 0.1875
- up_bias: float32 [4096], P('mp'), may hold values from -3 to 3
- down_proj: bfloat16 [4096, 1024], P('mp'), may hold values from -0.09375 to 0.09375
- down_bias: float32 [1024], replicated, may hold values from -3 to 3
- ffn_gain: float32 [1024], replicated, may hold values from 0.25 to 1.75
- ffn_shift: float32 [1024], replicated, may hold values from -3 to 3
- segments: int32 [8, 2048], P('dp'), may hold values from 0 to 128, as said below
- padding: int32 [8, 2048], P('dp'), may hold values from 0 to 1, as said below
- cotangent: bfloat16 [16384, 1024], P(('dp', 'mp')), may hold values from -6 to 6
Outputs:
- outputs: bfloat16 [16384, 1024], P(('dp', 'mp'))
- inputs_grad: bfloat16 [16384, 1024], P(('dp', 'mp'))
- in_proj_grad: float32 [3, 1024, 1024], P(None, None, 'mp')
- qv_bias_grad: float32 [2, 1024], P(None, 'mp')
- out_proj_grad: float32 [1024, 1024], P('mp')
- out_bias_grad: float32 [1024], replicated
- attn_gain_grad: float32 [1024], replicated
- attn_shift_grad: float32 [1024], replicated
- up_proj_grad: float32 [1024, 4096], P(None, 'mp')
- up_bias_grad: float32 [4096], P('mp')
- down_proj_grad: float32 [4096, 1024], P('mp')
- down_bias_grad: float32 [1024], replicated
- ffn_gain_grad: float32 [1024], replicated
- ffn_shift_grad: float32 [1024], replicated
Inputs may be any that keep to these rules, and one draw needn't show every extreme that they name: `segments`: within a row, segment numbers start at 0, never fall, and change only at positions that are multiples of 16, at least once in every 256 positions; the last position of every row alone holds 128. Each row ends in 1 to 128 padding positions; all others are real.
All inputs are finite; a program needn't handle non-finite values.
Results may differ from a plain program's by a relative error of at most 0.02.
Values may be sent and summed in bfloat16 or wider, within the bound.
A program may use at most 192 MiB of HBM per device.

v0:
```python
from functools import partial
import math

import jax
import jax.numpy as jnp
from jax import lax
from jax.experimental import pallas as pl
from jax.experimental.pallas import tpu as pltpu
from jax.sharding import PartitionSpec as P

HEAD = 64
BLOCK = 256
CHUNKS = 4
SMALL_TURNS = (0, 1, 3, 10, 16, 23, 23, 23, 23)
ORDERS = (
    (1, 2, 0),
    (0, 1, 2),
    (0, 1, 2),
    (0, 1, 2),
    (0, 1, 2),
    (0, 1, 2),
    (0, 1, 2),
    (0, 1, 2),
    (1, 2, 0),
    (0, 1, 2),
    (0, 1, 2),
    (0, 1, 2),
)
PLAN = {
    -1: ((2, 0), (1, 0), (0, 0), (3, 0),),
    0: ((7, 0), (0, 1), (2, 1), (4, 0),),
    1: ((5, 0), (6, 0),),
    3: ((1, 1), (0, 2),),
    4: ((2, 2), (3, 1), (1, 2),),
    5: ((7, 1), (2, 3), (3, 2),),
    6: ((1, 3), (4, 1), (7, 2), (2, 4),),
    7: ((3, 3), (5, 1), (1, 4), (4, 2),),
    8: ((11, 0), (0, 3), (2, 5), (6, 1), (7, 3),),
    10: ((3, 4),),
    12: ((5, 2),),
    14: ((1, 5),),
    15: ((4, 3),),
    16: ((11, 1),),
    17: ((0, 4), (6, 2),),
    18: ((7, 4),),
    19: ((3, 5),),
    20: ((5, 3),),
    21: ((4, 4),),
    23: ((11, 2),),
    25: ((0, 5),),
    26: ((6, 3),),
    28: ((7, 5),),
    29: ((5, 4),),
    32: ((10, 0), (11, 3), (1, 6), (2, 6), (3, 6), (4, 5), (8, 0), (9, 0), (0, 6), (7, 6), (6, 4), (5, 5), (-1, 0), (10, 1), (11, 4), (8, 1), (-1, 1), (4, 6), (6, 5), (10, 2), (9, 1), (11, 5), (-1, 2), (8, 2), (10, 3), (5, 6), (9, 2), (-1, 3), (6, 6), (10, 4), (9, 3), (8, 3), (11, 6), (9, 4), (8, 4), (10, 5), (9, 5), (8, 5), (10, 6), (9, 6), (8, 6),),
}
COLS = 256
UNPACK = 512
VMEM = 60 * 2**20
REMOTE = pl.BlockSpec(memory_space=pl.ANY)
LOCAL = pl.BlockSpec(memory_space=pltpu.VMEM)
MESH = pl.DeviceIdType.MESH


EPSILON = 1e-05


NEG = -1e30


def _head_masks(heads, width, value):
    lane = lax.broadcasted_iota(jnp.int32, (1, width), 1) // HEAD
    return [jnp.where(lane == h, value, 0.0).astype(jnp.bfloat16) for h in range(heads)]


def _nt(a, b):
    return lax.dot_general(a, b, (((1,), (1,)), ((), ())), preferred_element_type=jnp.float32)


def _tn(a, b):
    return lax.dot_general(a, b, (((0,), (0,)), ((), ())), preferred_element_type=jnp.float32)


def _nn(a, b):
    return jnp.dot(a, b, preferred_element_type=jnp.float32)


def _column(row):
    wide = jnp.broadcast_to(row.astype(jnp.float32), (128, row.shape[1])).T.astype(jnp.int32)
    return jnp.concatenate([wide] * (BLOCK // 128), axis=1)


def _bias(seg_ref, pad_ref, query_rows, key_rows):
    seg_q, pad_q = seg_ref[:, query_rows], pad_ref[:, query_rows]
    seg_k, pad_k = _column(seg_ref[:, key_rows]), _column(pad_ref[:, key_rows])
    allowed = (seg_k == seg_q) & ((pad_k > 0) | (pad_q == 0))
    return jnp.where(allowed, 0.0, NEG).astype(jnp.float32)


def _loop(count, body):
    def step(i, carry):
        body(i)
        return carry

    lax.fori_loop(0, count, step, 0)


def segment_places(segments, padding):
    row_count, seq_len = segments.shape
    if row_count > 1:
        segments = segments + jnp.arange(row_count, dtype=jnp.int32)[:, None] * (seq_len + 1)
    return segments.reshape(1, -1), padding.reshape(1, -1)


def _partners():
    me = lax.axis_index("mp")
    core = lax.rem(me, 2)
    sib = me + 1 - 2 * core
    cnt = lax.rem(me + 2, 4)
    dia = lax.rem(cnt + 1, 2) + cnt - lax.rem(cnt, 2)
    return me, sib, cnt, dia


def _remote(src, dst, send, recv, target):
    return pltpu.make_async_remote_copy(
        src_ref=src, dst_ref=dst, send_sem=send, recv_sem=recv, device_id=target, device_id_type=MESH
    )


def _greet(targets):
    barrier = pltpu.get_barrier_semaphore()
    for target in targets:
        pl.semaphore_signal(barrier, inc=1, device_id=target, device_id_type=MESH)
    pl.semaphore_wait(barrier, len(targets))


def _rows(start, size):
    return pl.ds(pl.multiple_of(start, size), size)


def _part(start, size):
    return pl.ds(pl.multiple_of(start, 16), size)


class Gather:
    def __init__(self, buffer, send, recv, stage, size, sib, cnt):
        self.buffer, self.send, self.recv = buffer, send, recv
        self.stage, self.size, self.sib, self.cnt = stage, size, sib, cnt

    def slot(self, r, k):
        return self.buffer.at[_rows((r * 4 + k) * self.size, self.size)]

    def copy(self, r, kind):
        src, dst, target = ((0, 1, self.sib), (0, 2, self.cnt), (2, 3, self.sib))[kind]
        return _remote(
            self.slot(r, src),
            self.slot(r, dst),
            self.send.at[self.stage, kind, r],
            self.recv.at[self.stage, kind, r],
            {"mp": target},
        )

    def start(self, r):
        self.copy(r, 1).start()
        self.copy(r, 0).start()

    def forward(self, r):
        self.copy(r, 1).wait_recv()
        self.copy(r, 2).start()

    def arrive(self, r):
        self.copy(r, 0).wait_recv()
        self.copy(r, 2).wait_recv()

    def sent(self, r):
        for kind in range(3):
            self.copy(r, kind).wait_send()


class Scatter:
    def __init__(self, bufs, send, recv, stage, size, sib, cnt):
        self.own, self.other, self.stage_sib, self.stage_x, self.recv_sib, self.recv_x = bufs
        self.send, self.recv = send, recv
        self.stage, self.size, self.sib, self.cnt = stage, size, sib, cnt

    def copy(self, r, kind):
        rows = _rows(r * self.size, self.size)
        src, dst, target = (
            (self.stage_sib.at[0, rows], self.recv_sib.at[0, rows], self.sib),
            (self.stage_sib.at[1, rows], self.recv_sib.at[1, rows], self.sib),
            (self.stage_x.at[rows], self.recv_x.at[rows], self.cnt),
        )[kind]
        return _remote(
            src, dst, self.send.at[self.stage, kind, r], self.recv.at[self.stage, kind, r], {"mp": target}
        )

    def sent(self, r):
        for kind in range(3):
            self.copy(r, kind).wait_send()

    def project(self, r, tile):
        size = self.size
        rows = _rows(r * size, size)

        def column(n, carry):
            cols = _rows(n * COLS, COLS)
            part = tile(cols)
            self.own[rows, cols] = part[:size]
            self.stage_sib[1, rows, cols] = part[size : 2 * size].astype(jnp.bfloat16)
            self.other[rows, cols] = part[2 * size : 3 * size]
            self.stage_sib[0, rows, cols] = part[3 * size :].astype(jnp.bfloat16)
            return carry

        lax.fori_loop(0, self.own.shape[1] // COLS, column, 0)
        self.copy(r, 0).start()
        self.copy(r, 1).start()

    def finish(self, r):
        rows = _rows(r * self.size, self.size)
        self.copy(r, 0).wait_recv()
        self.stage_x[rows, :] = (
            self.other[rows, :] + self.recv_sib[0, rows, :].astype(jnp.float32)
        ).astype(jnp.bfloat16)
        self.copy(r, 2).start()
        self.copy(r, 1).wait_recv()
        self.own[rows, :] += self.recv_sib[1, rows, :].astype(jnp.float32)

    def result(self, r):
        rows = _rows(r * self.size, self.size)
        self.copy(r, 2).wait_recv()
        return self.own[rows, :] + self.recv_x[rows, :].astype(jnp.float32)


def _scatter_scratch(own, width):
    f32, bf16 = jnp.float32, jnp.bfloat16
    return [
        pltpu.VMEM((own, width), f32),
        pltpu.VMEM((own, width), f32),
        pltpu.VMEM((2, own, width), bf16),
        pltpu.VMEM((own, width), bf16),
        pltpu.VMEM((2, own, width), bf16),
        pltpu.VMEM((own, width), bf16),
    ]


def _norm(summed):
    center = summed - jnp.mean(summed, axis=-1, keepdims=True)
    variance = jnp.mean(center * center, axis=-1, keepdims=True)
    inverse = lax.rsqrt(variance + EPSILON)
    return center * inverse, inverse


def _norm_back(scaled, unit, inverse):
    return inverse * (
        scaled
        - jnp.mean(scaled, axis=-1, keepdims=True)
        - unit * jnp.mean(scaled * unit, axis=-1, keepdims=True)
    )


class Reduce:
    def __init__(self, n, rows, order, source, work, final, sems):
        self.n, self.rows, self.source, self.work, self.final, self.sems = n, rows, source, work, final, sems
        self.steps = len(order)
        dp = lax.axis_index("dp")
        self.bit = [lax.rem(dp // (1 << b), 2) for b in order]
        self.peer = [{"dp": dp + (1 << b) * (1 - 2 * bit)} for b, bit in zip(order, self.bit)]

    def size(self, s):
        return self.rows >> s

    def start(self, s):
        first = self.n * self.rows
        for t in range(s):
            first = first + self.bit[t] * self.size(t + 1)
        return first

    def held(self, s):
        if s == 0:
            return self.source
        stride = self.rows - self.size(self.steps)
        return self.work, self.n * stride + self.rows - 2 * self.size(s)

    def halve(self, s):
        ref, first = self.held(s)
        half = self.size(s + 1)
        there, place = self.held(s + 1)
        return _remote(
            ref.at[_part(first + (1 - self.bit[s]) * half, half)],
            there.at[_part(place, half)],
            self.sems.at[0, self.n, s],
            self.sems.at[1, self.n, s],
            self.peer[s],
        )

    def double(self, s):
        block = self.final.at[_rows(self.start(s + 1), self.size(s + 1))]
        k = 2 * self.steps - 1 - s
        return _remote(block, block, self.sems.at[0, self.n, k], self.sems.at[1, self.n, k], self.peer[s])

    def step(self, k):
        steps = self.steps
        if 0 < k <= steps:
            s = k - 1
            half = self.size(s + 1)
            self.halve(s).wait_recv()
            ref, first = self.held(s)
            there, place = self.held(s + 1)
            total = there[_part(place, half), :].astype(jnp.float32) + ref[
                _part(first + self.bit[s] * half, half), :
            ].astype(jnp.float32)
            if k < steps:
                there[_part(place, half), :] = total.astype(jnp.bfloat16)
            else:
                self.final[_rows(self.start(steps), half), :] = total.astype(jnp.bfloat16)
        if k > steps:
            self.double(2 * steps - k).wait_recv()
        if k < steps:
            self.halve(k).start()
        elif k < 2 * steps:
            self.double(2 * steps - 1 - k).start()

    def sent(self):
        for s in range(self.steps):
            if s:
                self.halve(s).wait_send()
            self.double(s).wait_send()


def main_kernel(bits, pieces, *refs):
    f32, bf16 = jnp.float32, jnp.bfloat16
    (inputs_hbm, in_proj_hbm, out_proj_hbm, up_hbm, down_hbm, cotangent_hbm,
     qv_bias_ref, seg_ref, pad_ref, up_bias_ref, *refs) = refs
    vectors, refs = [v[...] for v in refs[:6]], refs[6:]
    out_bias, attn_gain, attn_shift, down_bias, ffn_gain, ffn_shift = vectors
    (outputs_hbm, inputs_grad_hbm, final_hbm, tokens_hbm, qkv_hbm, full_hbm, context_hbm, small_ref,
     context_ref, out_proj_ref, inputs_ref, up_ref, down_ref,
     weight_grads, normed_full, grad2_full, grad1_full, active, back, unit1, inverse1, grad_own, dots_ref,
     lse_ref, peak_ref, total_ref,
     own_acc, other_acc, stage_sib, stage_x, recv_sib, recv_x, work, final, small_recv, late_ref, late_recv,
     load_sems, block_sems, trade_sems, store_sems, final_sems, gather_send, gather_recv, scatter_send, scatter_recv,
     sems, small_sems, token_sems, keep_sems, full_sems) = refs
    outputs_ref = inputs_ref
    me, sib, cnt, dia = _partners()
    own, depth = inputs_ref.shape
    units, width = up_ref.shape[1], out_proj_ref.shape[0]
    length = 4 * own
    heads, token_blocks = width // HEAD, length // BLOCK
    size, whole = own // CHUNKS, length // CHUNKS
    blocks = (me, sib, cnt, dia)
    early = pieces == CHUNKS
    loop = partial(_loop, CHUNKS)

    def context_load(r):
        return [
            pltpu.make_async_copy(
                context_hbm.at[_rows(b * own + r * size, size)],
                context_ref.at[_rows((r * 4 + k) * size, size)],
                block_sems.at[k, r],
            )
            for k, b in enumerate(blocks)
        ]

    loads = [
        pltpu.make_async_copy(source, target, load_sems.at[k])
        for k, (source, target) in enumerate(
            (
                (out_proj_hbm, out_proj_ref),
                (inputs_hbm, inputs_ref),
                (up_hbm, up_ref),
                (down_hbm, down_ref),
                (cotangent_hbm, inputs_ref),
                (qkv_hbm, active.at[:, : 3 * width]),
                (tokens_hbm, normed_full),
                (context_hbm, back.at[:, width : 2 * width]),
                (full_hbm, grad1_full.at[:depth]),
                *[(in_proj_hbm.at[j], up_ref.at[:, j * width : (j + 1) * width]) for j in range(3)],
            )
        )
    ]
    own_context = pltpu.make_async_copy(
        back.at[_rows(me * own, own), :width], recv_x.at[:, _rows(me * width, width)], load_sems.at[12]
    )

    def trade(r, k):
        return _remote(
            back.at[_rows(blocks[k] * own + r * size, size), :width],
            recv_x.at[_rows(r * size, size), _rows(me * width, width)],
            trade_sems.at[0, k - 1, r],
            trade_sems.at[1, k - 1, r],
            {"mp": blocks[k]},
        )

    tokens_ref = normed_full

    def token_copy(r, kind):
        here = inputs_hbm.at[_rows(r * size, size)]
        place = _rows((cnt if kind == 2 else me) * own + r * size, size)
        src, target = ((here, sib), (here, cnt), (tokens_ref.at[place], sib))[kind]
        return _remote(
            src, tokens_ref.at[place], token_sems.at[0, kind, r], token_sems.at[1, kind, r], {"mp": target}
        )

    def keeps(k, r):
        place = _rows(blocks[k] * own + r * size, size)
        return [
            pltpu.make_async_copy(tokens_ref.at[place], tokens_hbm.at[place], keep_sems.at[0, k, r]),
            pltpu.make_async_copy(
                active.at[place, : 3 * width], qkv_hbm.at[place], keep_sems.at[1, k, r]
            ),
        ]

    dp = lax.axis_index("dp")
    shares = min(bits, (width // 16).bit_length() - 1)
    bit = [lax.rem(dp // (1 << b), 2) for b in range(bits)]
    over = [{"dp": dp + (1 << b) * (1 - 2 * bit[b])} for b in range(bits)]

    def span(block, s):
        first = block * width
        for t in range(s):
            first = first + bit[t] * (width >> (t + 1))
        return full_hbm.at[_part(first, width >> s)]

    def full_copy(k):
        if k == 0:
            pair = out_proj_hbm, span(me, 0), {"mp": sib}
        elif k == 1:
            first = sum(bit[t] * (width >> (t + 1)) for t in range(shares))
            pair = out_proj_hbm.at[_part(first, width >> shares)], span(me, shares), {"mp": cnt}
        elif k < 2 + shares:
            block = span(cnt, shares - (k - 2))
            pair = block, block, over[shares - 1 - (k - 2)]
        else:
            block = span(cnt, 0)
            pair = block, block, {"mp": sib}
        return _remote(pair[0], pair[1], full_sems.at[0, k], full_sems.at[1, k], pair[2])

    own_quarter = pltpu.make_async_copy(out_proj_hbm, span(me, 0), load_sems.at[13])
    own_tokens = pltpu.make_async_copy(inputs_hbm, tokens_ref.at[_rows(me * own, own)], load_sems.at[14])

    def full_step(k):
        full_copy(k).wait_recv()
        full_copy(k + 1).start()

    def store(k, r):
        rows = _rows(r * size, size)
        target = (outputs_hbm, inputs_grad_hbm)[k]
        return pltpu.make_async_copy(outputs_ref.at[rows], target.at[rows], store_sems.at[k, r])

    bufs = (own_acc, other_acc, stage_sib, stage_x, recv_sib, recv_x)
    gathers = [
        Gather(buf, gather_send, gather_recv, stage, size, sib, cnt)
        for stage, buf in enumerate((normed_full, grad2_full, grad1_full))
    ]
    scatters = [
        Scatter(bufs, scatter_send, scatter_recv, stage, size, sib, cnt) for stage in range(4)
    ]
    piece = depth // pieces
    count = 3 * pieces

    def source(n):
        if early and n == count - 1:
            return outputs_ref, 0
        return weight_grads, (n if n < 2 * pieces else n - 2 * pieces) * piece

    sums = [
        Reduce(
            n, piece, ORDERS[n] if early else tuple(range(bits)), source(n), work, final, sems
        )
        for n in range(count)
    ]
    for load in (*loads[9:], own_tokens, loads[1], own_quarter):
        load.start()
    small_ref[...] = jnp.zeros_like(small_ref)
    late_ref[...] = jnp.zeros_like(late_ref)
    _greet([{"mp": sib}, {"mp": cnt}, {"mp": dia}, *over])
    full_copy(1).start()
    for r in range(CHUNKS):
        token_copy(r, 1).start()
        token_copy(r, 0).start()
    full_copy(0).start()
    for load in (loads[0], loads[3]):
        load.start()

    def project(k, r):
        place = _rows(blocks[k] * own + r * size, size)
        part = _nn(tokens_ref[place, :], up_ref[:, : 3 * width])
        active[place, :width] = (part[:, :width] + qv_bias_ref[:1, :]).astype(bf16)
        active[place, width : 2 * width] = part[:, width : 2 * width].astype(bf16)
        active[place, 2 * width : 3 * width] = (part[:, 2 * width :] + qv_bias_ref[1:, :]).astype(bf16)
        for keep in keeps(k, r):
            keep.start()

    for load in loads[9:]:
        load.wait()
    own_tokens.wait()
    loop(lambda r: project(0, r))
    full_step(1)

    def sib_part(r):
        token_copy(r, 0).wait_recv()
        project(1, r)

    loop(sib_part)
    full_step(2)

    scaled = _head_masks(heads, width, 1.0 / math.sqrt(HEAD))
    plain = _head_masks(heads, width, 1.0)

    def attention(i):
        query_rows = _rows(i * BLOCK, BLOCK)
        acc = own_acc.at[:width, :BLOCK]
        peak_ref[...] = jnp.full_like(peak_ref, 2 * NEG)
        total_ref[...] = jnp.zeros_like(total_ref)
        acc[...] = jnp.zeros_like(acc)

        def meet(j, carry):
            rows = _rows(j * BLOCK, BLOCK)
            bias = _bias(seg_ref, pad_ref, query_rows, rows)
            query, key = active[query_rows, :width], active[rows, width : 2 * width]
            value = active[rows, 2 * width : 3 * width].T
            for h in range(heads):
                scores = _nt(key, query * scaled[h]) + bias
                old = peak_ref[h]
                peak = jnp.maximum(old, jnp.max(scores, axis=0, keepdims=True))
                expo = jnp.exp(scores - peak)
                ratio = jnp.exp(old - peak)
                peak_ref[h] = peak
                total_ref[h] = total_ref[h] * ratio + jnp.sum(expo, axis=0, keepdims=True)
                place = pl.ds(h * HEAD, HEAD)
                acc[place, :] = acc[place, :] * ratio + _nn(
                    value[h * HEAD : (h + 1) * HEAD], expo.astype(bf16)
                )
            return carry

        lax.fori_loop(jnp.maximum(i - 1, 0), jnp.minimum(i + 2, token_blocks), meet, 0)
        for h in range(heads):
            place = pl.ds(h * HEAD, HEAD)
            acc[place, :] = acc[place, :] / total_ref[h]
            lse_ref[h : h + 1, query_rows] = peak_ref[h] + jnp.log(total_ref[h])
        back[query_rows, :width] = acc[...].astype(bf16).T

    half = token_blocks // 2
    chip = me // 2
    per_device = own // BLOCK
    chunks_per = BLOCK // size

    def near(p):
        attention(jnp.where(chip == 0, p, token_blocks - 1 - p))

    _loop(half - 1, near)

    def far_part(r):
        @pl.when(r == 0)
        def _():
            full_step(3)

        @pl.when(r == 2)
        def _():
            for k in range(4, shares + 2):
                full_step(k)

        token_copy(r, 1).wait_recv()
        token_copy(r, 2).start()
        project(2, r)
        token_copy(r, 2).wait_recv()
        project(3, r)

    loop(far_part)
    loads[2].start()
    full_copy(0).wait_recv()
    full_copy(shares + 2).wait_recv()
    own_quarter.wait()
    loads[8].start()

    def tokens_done(r):
        for kind in range(3):
            token_copy(r, kind).wait_send()
        for k in range(4):
            keeps(k, r)[0].wait()

    def far(p):
        k, h = lax.rem(p, 2), p // 2
        attention(jnp.where(k == 0, cnt, dia) * per_device + h)

        @pl.when(p == 0)
        def _():
            loop(tokens_done)

        for c in range(2):

            @pl.when(k == c)
            def _():
                for t in range(chunks_per):
                    trade(h * chunks_per + t, 2 + c).start()

    _loop(2 * per_device, far)
    attention(jnp.where(chip == 0, half - 1, half))
    loop(lambda r: trade(r, 1).start())
    own_context.start()
    save_context = pltpu.make_async_copy(back.at[:, :width], context_hbm, load_sems.at[15])
    save_context.start()

    def add_sum(k, value):
        small_ref[k : k + 1, :] += jnp.sum(value, axis=0, keepdims=True)

    own_context.wait()
    loads[1].wait()
    loads[8].wait()

    def lower_norm(r):
        rows = _rows(r * size, size)
        for k in (1, 2, 3):
            trade(r, k).wait_recv()
        attended = _nn(recv_x[rows, :], grad1_full[:depth, :])
        unit, inverse = _norm(inputs_ref[rows, :].astype(f32) + attended + out_bias)
        unit1[rows, :] = unit
        inverse1[rows, :] = inverse
        gathers[0].slot(r, 0)[...] = (unit * attn_gain + attn_shift).astype(bf16)
        gathers[0].start(r)

    loop(lower_norm)
    loads[4].start()
    save_context.wait()
    for k in range(shares + 3):
        full_copy(k).wait_send()

    def front_done(r):
        for k in range(4):
            keeps(k, r)[1].wait()
        for k in (1, 2, 3):
            trade(r, k).wait_send()
        for load in context_load(r):
            load.start()

    loop(front_done)
    loads[2].wait()
    loads[3].wait()

    def feed_forward(r):
        rows = _rows(r * whole, whole)
        gathers[0].forward(r)
        gathers[0].arrive(r)

        def column(n, carry):
            cols = _rows(n * COLS, COLS)
            upper = _nn(normed_full[rows, :], up_ref[:, cols]) + up_bias_ref[:, cols]
            cdf = 0.5 + 0.5 * lax.erf(upper * math.sqrt(0.5))
            pdf = jnp.exp(upper * upper * -0.5) * (1.0 / math.sqrt(2.0 * math.pi))
            active[rows, cols] = (upper * cdf).astype(bf16)
            back[rows, cols] = (cdf + upper * pdf).astype(bf16)
            return carry

        lax.fori_loop(0, units // COLS, column, 0)
        scatters[1].project(r, lambda cols: _nn(active[rows, :], down_ref[:, cols]))
        scatters[1].finish(r)

    loop(feed_forward)
    loads[4].wait()

    def upper_norm(r):
        rows = _rows(r * size, size)
        normed = unit1[rows, :] * attn_gain + attn_shift
        unit, inverse = _norm(normed + scatters[1].result(r) + down_bias)
        cotangent = inputs_ref[rows, :].astype(f32)
        outputs_ref[rows, :] = (unit * ffn_gain + ffn_shift).astype(bf16)
        store(0, r).start()
        grad = _norm_back(cotangent * ffn_gain, unit, inverse)
        gathers[1].slot(r, 0)[...] = grad.astype(bf16)
        gathers[1].start(r)
        grad_own[rows, :] = grad
        add_sum(3, grad)
        add_sum(4, cotangent * unit)
        add_sum(5, cotangent)

    loop(upper_norm)

    def take(r):
        gathers[1].forward(r)
        gathers[1].arrive(r)
        scatters[1].sent(r)

    def feed_back(r):
        rows = _rows(r * whole, whole)

        def column(n, carry):
            cols = _rows(n * COLS, COLS)
            incoming = _nt(grad2_full[rows, :], down_ref[cols, :])
            upper_back = (back[rows, cols].astype(f32) * incoming).astype(bf16)
            back[rows, cols] = upper_back
            late_ref[1:2, cols] += jnp.sum(upper_back.astype(f32), axis=0, keepdims=True)
            return carry

        lax.fori_loop(0, units // COLS, column, 0)
        scatters[2].project(r, lambda cols: _nt(back[rows, :], up_ref[cols, :]))
        scatters[2].finish(r)

    def take_back(r):
        take(r)
        feed_back(r)

    _loop(CHUNKS - 1, take_back)
    take(CHUNKS - 1)

    def weights(k, p):
        cols = _rows(p * (depth // CHUNKS), depth // CHUNKS)
        place = _rows(k * depth + p * (depth // CHUNKS), depth // CHUNKS)
        if k == 0:
            weight_grads[place, :] = _tn(active[:, cols], grad2_full[...]).astype(bf16)
        else:
            weight_grads[place, :] = _tn(normed_full[:, cols], back[...]).astype(bf16)

    def out_weights():
        target = outputs_ref.at[:width] if early else weight_grads.at[3 * width : 4 * width]
        target[...] = _tn(context_ref[...], grad1_full[...]).astype(bf16)

    def in_weights(j):
        weight_grads[_rows(j * width, width), :] = _tn(
            grads[:, j * width : (j + 1) * width], normed_full[...]
        ).astype(bf16)

    def move(n, k):
        if k == 0 and n < 2 * pieces:
            weights(n // pieces, n % pieces)
        elif k == 0 and n == count - 1:
            out_weights()
        elif k == 0:
            in_weights(n - 2 * pieces)
        sums[n].step(k)
        if k == 2 * bits:
            store_final(n).start()

    def store_final(n):
        rows = _rows(n * piece, piece)
        return pltpu.make_async_copy(final.at[rows], final_hbm.at[rows], final_sems.at[n])

    def slot(i, first, number):
        for at in range(first, first + number) if early else ():
            if at in PLAN:

                @pl.when(i == at - first)
                def _():
                    for n, k in PLAN[at]:
                        move(n, k)

    if early:
        for n, k in PLAN[-1]:
            move(n, k)
    feed_back(CHUNKS - 1)
    for load in loads[9:]:
        load.start()

    def lower_back(r):
        slot(r, 0, CHUNKS)
        if not early:
            for k in range(2):

                @pl.when(r // 2 == k)
                def _():
                    for h in range(2):
                        weights(k, 2 * r - 4 * k + h)

                @pl.when(r == 2 * k + 1)
                def _():
                    sums[k].step(0)

        rows = _rows(r * size, size)
        incoming = grad_own[rows, :] + scatters[2].result(r)
        unit = unit1[rows, :]
        grad = _norm_back(incoming * attn_gain, unit, inverse1[rows, :])
        gathers[2].slot(r, 0)[...] = grad.astype(bf16)
        gathers[2].start(r)
        grad_own[rows, :] = grad
        add_sum(0, grad)
        add_sum(1, incoming * unit)
        add_sum(2, incoming)

    loop(lower_back)
    gathers_done = lambda r: [gather.sent(r) for gather in gathers[:2]]
    loop(gathers_done)
    for load in loads[5:8]:
        load.start()

    loads[0].wait()
    loop(lambda r: [load.wait() for load in context_load(r)])

    def context_back(r):
        slot(r, CHUNKS, CHUNKS)
        rows = _rows(r * whole, whole)
        gathers[2].forward(r)
        gathers[2].arrive(r)
        scatters[2].sent(r)
        grad = _nt(grad1_full[rows, :], out_proj_ref[...]).astype(bf16)
        for k, b in enumerate(blocks):
            part = _rows(b * own + r * size, size)
            back[part, :width] = grad[k * size : (k + 1) * size]

    loop(context_back)
    loop(lambda r: gathers[2].sent(r))
    loop(lambda r: store(0, r).wait())
    for load in loads[5:8]:
        load.wait()

    targets = [{"mp": sib}, {"mp": cnt}, *over]

    def small_step(k):
        return _remote(
            small_ref.at[:8], small_recv.at[k], small_sems.at[0, k], small_sems.at[1, k], targets[k]
        )

    def small_end(k):
        small_step(k).wait()
        small_ref[:8, :] += small_recv[k]

    def late_step(k):
        at = len(targets) + k
        return _remote(late_ref, late_recv.at[k], small_sems.at[0, at], small_sems.at[1, at], over[k])

    def late_end(k):
        late_step(k).wait()
        late_ref[...] += late_recv[k]

    def small_turn(k):
        if k:
            small_end(k - 1)
        if k < len(targets):
            small_step(k).start()

    keys_acc, values_acc, query_acc = unit1, other_acc, own_acc.at[:width, :BLOCK]
    keys_acc[...] = jnp.zeros_like(keys_acc)
    values_acc[...] = jnp.zeros_like(values_acc)
    grads = grad2_full
    per = own // BLOCK

    def spot(j):
        return _rows(lax.rem(j, per) * BLOCK, BLOCK), _rows(j // per * width, width)

    def attend(t):
        i, turn = t // 3, lax.rem(t, 3)
        for k in range(len(targets) + 1):

            @pl.when(t == SMALL_TURNS[k])
            def _():
                small_turn(k)

        slot(t, 2 * CHUNKS, 3 * token_blocks)
        query_rows = _rows(i * BLOCK, BLOCK)

        @pl.when(turn == 0)
        def _():
            product = (
                back[query_rows, :width].astype(f32) * back[query_rows, width : 2 * width].astype(f32)
            ).T
            for h in range(heads):
                dots_ref[h : h + 1, :] = jnp.sum(
                    product[h * HEAD : (h + 1) * HEAD], axis=0, keepdims=True
                )
            query_acc[...] = jnp.zeros_like(query_acc)

        @pl.when((i + turn >= 1) & (i + turn <= token_blocks))
        def _():
            j = jnp.clip(i + turn - 1, 0, token_blocks - 1)
            query, grad = active[query_rows, :width], back[query_rows, :width]
            rows = _rows(j * BLOCK, BLOCK)
            bias = _bias(seg_ref, pad_ref, query_rows, rows)
            key, value = active[rows, width : 2 * width], active[rows, 2 * width : 3 * width]
            key_rows = (key * (1.0 / math.sqrt(HEAD))).astype(bf16).T
            key_add = jnp.zeros((BLOCK, width), f32)
            value_add = jnp.zeros((BLOCK, width), f32)
            for h in range(heads):
                query_h, grad_h = query * scaled[h], grad * plain[h]
                scores = _nt(key, query_h) + bias
                prob = jnp.exp(scores - lse_ref[h : h + 1, query_rows])
                score_grad = (prob * (_nt(value, grad_h) - dots_ref[h : h + 1, :])).astype(bf16)
                key_add = key_add + _nn(score_grad, query_h)
                value_add = value_add + _nn(prob.astype(bf16), grad_h)
                query_acc[pl.ds(h * HEAD, HEAD), :] += _nn(key_rows[h * HEAD : (h + 1) * HEAD], score_grad)
            keys_acc[spot(j)] += key_add
            values_acc[spot(j)] += value_add

        @pl.when(turn == 2)
        def _():
            grads[query_rows, :width] = query_acc[...].astype(bf16).T

    _loop(3 * token_blocks, attend)

    def keep(j):
        rows = _rows(j * BLOCK, BLOCK)
        grads[rows, width : 2 * width] = keys_acc[spot(j)].astype(bf16)
        grads[rows, 2 * width : 3 * width] = values_acc[spot(j)].astype(bf16)

    _loop(token_blocks, keep)

    if not early:
        for n in range(2):
            sums[n].step(1)
        out_weights()
        in_weights(0)
        in_weights(1)
        in_weights(2)
    for n in range(2 * pieces):
        sums[n].halve(0).wait_send()

    def partial_rows(r):
        chunk = jnp.concatenate(
            [grads[_rows(b * own + r * size, size), : 3 * width] for b in blocks], axis=0
        )

        def tile(cols):
            return _nt(chunk, up_ref[cols, : 3 * width])

        scatters[3].project(r, tile)
        scatters[3].finish(r)

    def finish(r):
        rows = _rows(r * size, size)
        outputs_ref[rows, :] = (grad_own[rows, :] + scatters[3].result(r)).astype(bf16)
        store(1, r).start()
        scatters[3].sent(r)

    def bias(j):
        return jnp.sum(grads[:, j * width : (j + 1) * width].astype(f32), axis=0, keepdims=True)

    for load in loads[9:]:
        load.wait()
    late_ref[:1, :width] = bias(0)
    late_ref[:1, width : 2 * width] = bias(2)
    late_step(0).start()
    if early:
        tail = PLAN[2 * CHUNKS + 3 * token_blocks]
    else:
        tail = [(2, 0)] + [(-1, r) for r in range(CHUNKS)]
        tail += [(n, k) for k in range(1, 2 * bits + 1) for n in range(3) if n == 2 or k > 1]
    last = max(k for k, (n, _) in enumerate(tail) if n < 0)
    turns = [(len(tail) - 1) * (k + 2) // (bits + 1) for k in range(bits)]
    for at, (n, k) in enumerate(tail):
        if n < 0:
            partial_rows(k)
        elif k or early:
            move(n, k)
        else:
            sums[n].step(0)
        for turn in [turn for turn, place in enumerate(turns) if place == at]:
            late_end(turn)
            if turn + 1 < bits:
                late_step(turn + 1).start()
        if at == last + 3 * (len(tail) - 1 - last) // 4:
            if early:
                sums[-1].halve(0).wait_send()
            loop(finish)
    for n in range(count):
        sums[n].sent()
        if n >= 2 * pieces and not (early and n == count - 1):
            sums[n].halve(0).wait_send()
    small_ref[8:10, :] = late_ref[:2, :]
    loop(lambda r: store(1, r).wait())
    for n in range(3 * pieces):
        store_final(n).wait()


def main_layer(mesh, arrays, small_arrays):
    f32, bf16 = jnp.float32, jnp.bfloat16
    inputs, in_proj, out_proj, up_proj, down_proj, _ = arrays
    own, depth = inputs.shape
    units, width = up_proj.shape[1], out_proj.shape[0]
    whole, half = 4 * own, depth // 2
    bits = mesh.shape["dp"].bit_length() - 1
    pieces = CHUNKS if (depth // CHUNKS >> bits) >= 16 else 1
    outs = [
        ((own, depth), bf16),
        ((own, depth), bf16),
        ((3 * depth, depth), bf16),
        ((whole, depth), bf16),
        ((whole, 3 * width), bf16),
        ((4 * width, depth), bf16),
        ((whole, width), bf16),
        ((16, depth), f32),
    ]
    return pl.pallas_call(
        partial(main_kernel, bits, pieces),
        out_shape=[jax.ShapeDtypeStruct(*out) for out in outs],
        in_specs=[REMOTE] * 6 + [LOCAL] * 10,
        out_specs=[REMOTE] * 7 + [LOCAL],
        scratch_shapes=[
            pltpu.VMEM((whole, width), bf16),
            *[pltpu.VMEM(array.shape, bf16) for array in (out_proj, inputs, up_proj, down_proj)],
            pltpu.VMEM((2 * depth, depth), bf16),
            pltpu.VMEM((whole, depth), bf16),
            pltpu.VMEM((whole, depth), bf16),
            pltpu.VMEM((whole, depth), bf16),
            pltpu.VMEM((whole, units), bf16),
            pltpu.VMEM((whole, units), bf16),
            pltpu.VMEM((own, depth), f32),
            pltpu.VMEM((own, 1), f32),
            pltpu.VMEM((own, depth), f32),
            pltpu.VMEM((8, BLOCK), f32),
            pltpu.VMEM((8, whole), f32),
            pltpu.VMEM((width // HEAD, 1, BLOCK), f32),
            pltpu.VMEM((width // HEAD, 1, BLOCK), f32),
            *_scatter_scratch(own, depth),
            pltpu.VMEM((3 * pieces * (depth // pieces - (depth // pieces >> bits)), depth), bf16),
            pltpu.VMEM((3 * depth, depth), bf16),
            pltpu.VMEM((2 + bits, 8, depth), f32),
            pltpu.VMEM((8, depth), f32),
            pltpu.VMEM((bits, 8, depth), f32),
            pltpu.SemaphoreType.DMA((16,)),
            pltpu.SemaphoreType.DMA((4, CHUNKS)),
            pltpu.SemaphoreType.DMA((2, 3, CHUNKS)),
            pltpu.SemaphoreType.DMA((2, CHUNKS)),
            pltpu.SemaphoreType.DMA((3 * pieces,)),
            pltpu.SemaphoreType.DMA((3, 3, CHUNKS)),
            pltpu.SemaphoreType.DMA((3, 3, CHUNKS)),
            pltpu.SemaphoreType.DMA((4, 3, CHUNKS)),
            pltpu.SemaphoreType.DMA((4, 3, CHUNKS)),
            pltpu.SemaphoreType.DMA((2, 3 * pieces, 2 * bits)),
            pltpu.SemaphoreType.DMA((2, 2 + 2 * bits)),
            pltpu.SemaphoreType.DMA((2, 3, CHUNKS)),
            pltpu.SemaphoreType.DMA((2, 4, CHUNKS)),
            pltpu.SemaphoreType.DMA((2, 3 + bits)),
        ],
        compiler_params=pltpu.CompilerParams(
            collective_id=1, has_side_effects=True, vmem_limit_bytes=63 * 2**20
        ),
        name="main_layer",
    )(*arrays, *small_arrays)


def unpack_kernel(
    width, final_ref, attn_ref, small_ref, outputs_ref, inputs_grad_ref, down_ref, up_ref, in_ref, out_ref,
    qv_ref, up_bias_ref, *refs,
):
    f32 = jnp.float32
    vectors, outputs_out, inputs_grad_out = refs[:6], refs[6], refs[7]
    down_ref[...] = final_ref[0].astype(f32)
    up_ref[...] = final_ref[1].astype(f32)
    for j in range(3):
        in_ref[j] = attn_ref[j * width : (j + 1) * width, :].astype(f32).T
    out_ref[...] = attn_ref[3 * width :, :].astype(f32)
    outputs_out[...] = outputs_ref[...]
    inputs_grad_out[...] = inputs_grad_ref[...]
    for k, vector in enumerate(vectors):
        vector[...] = small_ref[k : k + 1, :]
    up_bias_ref[...] = small_ref[9:10, :]
    for k in range(2):
        qv_ref[k : k + 1, :] = small_ref[8:9, k * width : (k + 1) * width]


def unpack(final, small, outputs, inputs_grad, width):
    f32 = jnp.float32
    own, depth = outputs.shape
    steps = depth // UNPACK
    part = own // steps
    matrix = pl.BlockSpec((UNPACK, depth), lambda i: (i, 0))
    tokens = pl.BlockSpec((part, depth), lambda i: (i, 0))
    vector = pl.BlockSpec((1, depth), lambda i: (0, 0))
    shapes = [
        ((depth, depth), f32, matrix),
        ((depth, depth), f32, matrix),
        ((3, depth, width), f32, pl.BlockSpec((3, UNPACK, width), lambda i: (0, i, 0))),
        ((width, depth), f32, pl.BlockSpec((width, UNPACK), lambda i: (0, i))),
        ((2, width), f32, pl.BlockSpec((2, width), lambda i: (0, 0))),
        *[((1, depth), f32, vector)] * 7,
        ((own, depth), jnp.bfloat16, tokens),
        ((own, depth), jnp.bfloat16, tokens),
    ]
    return pl.pallas_call(
        partial(unpack_kernel, width),
        grid=(steps,),
        in_specs=[
            pl.BlockSpec((2, UNPACK, depth), lambda i: (0, i, 0)),
            pl.BlockSpec((depth, UNPACK), lambda i: (2, i)),
            pl.BlockSpec((16, depth), lambda i: (0, 0)),
            tokens,
            tokens,
        ],
        out_specs=[spec for _, _, spec in shapes],
        out_shape=[jax.ShapeDtypeStruct(shape, dtype) for shape, dtype, _ in shapes],
        compiler_params=pltpu.CompilerParams(vmem_limit_bytes=VMEM),
        name="unpack_gradients",
    )(final.reshape(3, depth, depth), final, small, outputs, inputs_grad)


def shards(
    mesh,
    inputs,
    in_proj,
    qv_bias,
    out_proj,
    out_bias,
    attn_gain,
    attn_shift,
    up_proj,
    up_bias,
    down_proj,
    down_bias,
    ffn_gain,
    ffn_shift,
    segments,
    padding,
    cotangent,
):
    places, real = segment_places(segments, padding)
    vectors = [v[None] for v in (out_bias, attn_gain, attn_shift, down_bias, ffn_gain, ffn_shift)]
    outputs, inputs_grad, final, _, _, _, _, small = main_layer(
        mesh,
        (inputs, in_proj, out_proj, up_proj, down_proj, cotangent),
        (qv_bias, places, real, up_bias[None], *vectors),
    )
    down_grad, up_grad, in_grad, out_grad, qv_grad, up_bias_grad, *vectors, outputs, inputs_grad = unpack(
        final, small, outputs, inputs_grad, in_proj.shape[2]
    )
    vectors = [v[0] for v in vectors]
    return (
        outputs,
        inputs_grad,
        in_grad,
        qv_grad,
        out_grad,
        *vectors[:3],
        up_grad,
        up_bias_grad[0],
        down_grad,
        *vectors[3:],
    )


def solution(mesh):
    return jax.shard_map(
        partial(shards, mesh),
        mesh=mesh,
        in_specs=(
            P(("dp", "mp"), None),
            P(None, None, "mp"),
            P(None, "mp"),
            P("mp", None),
            P(),
            P(),
            P(),
            P(None, "mp"),
            P("mp"),
            P("mp", None),
            P(),
            P(),
            P(),
            P("dp", None),
            P("dp", None),
            P(("dp", "mp"), None),
        ),
        out_specs=(
            P(("dp", "mp"), None),
            P(("dp", "mp"), None),
            P(None, None, "mp"),
            P(None, "mp"),
            P("mp", None),
            P(),
            P(),
            P(),
            P(None, "mp"),
            P("mp"),
            P("mp", None),
            P(),
            P(),
            P(),
        ),
        check_vma=False,
    )
```

profile of v0, /device:TPU:0, one launch (start us, length us, event | category | flops | bytes accessed | tf_op | source)
XLA Modules:
  0.0 275.6 jit_solution(14152079438102039820)
XLA Ops:
  0.7 266.9 %main_layer.1 = (bf16[512,1024]{1,0:T(8,128)(2,1)}, bf16[512,1024]{1,0:T(8,128)(2,1)}, bf16[3072,1024]{1,0:T(8,128)(2,1)}, bf16[2048,1024]{1,0:T(8,128)(2,1)}, b...) custom-call(bf16[512,1024]{1,0:T(8,128)(2,1)} %refs_0_.1, ...), custom_call_target="tpu_custom_call" | custom-call | tf_op jit(solution)/shard_map/main_layer/pallas_call | solution.py:978
  267.6 7.9 %unpack_gradients.1 = (f32[1024,1024]{1,0:T(8,128)}, f32[1024,1024]{1,0:T(8,128)}, f32[3,1024,256]{2,1,0:T(8,128)}, f32[256,1024]{1,0:T(8,128)}, f32[2,256]{1,0:...) custom-call(bf16[3,1024,1024]{2,1,0:T(8,128)(2,1)} %bitcast.15, ...), custom_call_target="tpu_custom_call" | custom-call | tf_op jit(solution)/shard_map/unpack_gradients/pallas_call | solution.py:1065
where the time goes:
time: 276 us
  Pallas kernels  275 us (100%)
    pallas_call x1, Pallas kernels, main_layer(): pl.pallas_call(partial(main_kernel, bits, pieces), out_shape=[jax.ShapeDt...  267 us
    pallas_call x1, Pallas kernels, unpack(): pl.pallas_call(partial(unpack_kernel, width), grid=(steps,), in_specs=[pl...  7.86 us

commit v1 on v0

--- a/solution.py
+++ b/solution.py
@@ -13,7 +13,8 @@
 CHUNKS = 4
 SMALL_TURNS = (0, 1, 3, 10, 16, 23, 23, 23, 23)
 ORDERS = (
-    (1, 2, 0),
+    (0, 1, 2),
+    (1, 0, 2),
     (0, 1, 2),
     (0, 1, 2),
     (0, 1, 2),
@@ -21,39 +22,38 @@
     (0, 1, 2),
     (0, 1, 2),
     (0, 1, 2),
-    (1, 2, 0),
     (0, 1, 2),
-    (0, 1, 2),
+    (1, 0, 2),
     (0, 1, 2),
 )
 PLAN = {
-    -1: ((2, 0), (1, 0), (0, 0), (3, 0),),
-    0: ((7, 0), (0, 1), (2, 1), (4, 0),),
-    1: ((5, 0), (6, 0),),
-    3: ((1, 1), (0, 2),),
-    4: ((2, 2), (3, 1), (1, 2),),
-    5: ((7, 1), (2, 3), (3, 2),),
-    6: ((1, 3), (4, 1), (7, 2), (2, 4),),
-    7: ((3, 3), (5, 1), (1, 4), (4, 2),),
-    8: ((11, 0), (0, 3), (2, 5), (6, 1), (7, 3),),
-    10: ((3, 4),),
-    12: ((5, 2),),
-    14: ((1, 5),),
-    15: ((4, 3),),
-    16: ((11, 1),),
-    17: ((0, 4), (6, 2),),
-    18: ((7, 4),),
-    19: ((3, 5),),
-    20: ((5, 3),),
-    21: ((4, 4),),
-    23: ((11, 2),),
-    25: ((0, 5),),
-    26: ((6, 3),),
-    28: ((7, 5),),
-    29: ((5, 4),),
-    32: ((10, 0), (11, 3), (1, 6), (2, 6), (3, 6), (4, 5), (8, 0), (9, 0), (0, 6), (7, 6), (6, 4), (5, 5), (-1, 0), (10, 1), (11, 4), (8, 1), (-1, 1), (4, 6), (6, 5), (10, 2), (9, 1), (11, 5), (-1, 2), (8, 2), (10, 3), (5, 6), (9, 2), (-1, 3), (6, 6), (10, 4), (9, 3), (8, 3), (11, 6), (9, 4), (8, 4), (10, 5), (9, 5), (8, 5), (10, 6), (9, 6), (8, 6),),
+    -1: ((3, 0), (1, 0), (2, 0), (0, 0),),
+    0: ((5, 0), (1, 1), (3, 1), (4, 0),),
+    1: ((7, 0), (6, 0), (2, 1),),
+    3: ((3, 2),),
+    4: ((0, 1), (2, 2), (3, 3),),
+    5: ((5, 1), (0, 2), (2, 3), (1, 2),),
+    6: ((3, 4), (5, 2), (4, 1), (0, 3),),
+    7: ((2, 4), (1, 3), (7, 1), (3, 5),),
+    8: ((11, 0), (4, 2), (5, 3),),
+    9: ((6, 1),),
+    10: ((0, 4),),
+    12: ((2, 5),),
+    14: ((1, 4),),
+    16: ((7, 2),),
+    17: ((4, 3),),
+    19: ((11, 1), (5, 4),),
+    21: ((6, 2),),
+    24: ((0, 5),),
+    25: ((7, 3),),
+    26: ((4, 4),),
+    27: ((1, 5),),
+    29: ((11, 2),),
+    31: ((5, 5),),
+    32: ((10, 0), (6, 3), (7, 4), (0, 6), (2, 6), (3, 6), (8, 0), (4, 5), (9, 0), (-1, 0), (1, 6), (5, 6), (-1, 1), (11, 3), (-1, 2), (8, 1), (-1, 3), (10, 1), (6, 4), (4, 6), (7, 5), (11, 4), (8, 2), (9, 1), (6, 5), (10, 2), (11, 5), (8, 3), (7, 6), (9, 2), (10, 3), (8, 4), (6, 6), (9, 3), (11, 6), (10, 4), (8, 5), (9, 4), (9, 5), (10, 5), (8, 6), (10, 6), (9, 6),),
 }
 COLS = 256
+PART = 256
 UNPACK = 512
 VMEM = 60 * 2**20
 REMOTE = pl.BlockSpec(memory_space=pl.ANY)
@@ -329,16 +329,20 @@
 def main_kernel(bits, pieces, *refs):
     f32, bf16 = jnp.float32, jnp.bfloat16
     (inputs_hbm, in_proj_hbm, out_proj_hbm, up_hbm, down_hbm, cotangent_hbm,
-     qv_bias_ref, seg_ref, pad_ref, up_bias_ref, *refs) = refs
-    vectors, refs = [v[...] for v in refs[:6]], refs[6:]
-    out_bias, attn_gain, attn_shift, down_bias, ffn_gain, ffn_shift = vectors
+     *refs) = refs
+    small_hbm, refs = refs[:10], refs[10:]
     (outputs_hbm, inputs_grad_hbm, final_hbm, tokens_hbm, qkv_hbm, full_hbm, context_hbm, small_ref,
      context_ref, out_proj_ref, inputs_ref, up_ref, down_ref,
      weight_grads, normed_full, grad2_full, grad1_full, active, back, unit1, inverse1, grad_own, dots_ref,
      lse_ref, peak_ref, total_ref,
      own_acc, other_acc, stage_sib, stage_x, recv_sib, recv_x, work, final, small_recv, late_ref, late_recv,
      load_sems, block_sems, trade_sems, store_sems, final_sems, gather_send, gather_recv, scatter_send, scatter_recv,
-     sems, small_sems, token_sems, keep_sems, full_sems) = refs
+     sems, small_sems, token_sems, keep_sems, full_sems, operand_sems, *small_operands) = refs
+    qv_bias_ref, seg_ref, pad_ref, up_bias_ref, *vector_refs = small_operands
+    small_loads = [
+        pltpu.make_async_copy(source, target, operand_sems.at[k])
+        for k, (source, target) in enumerate(zip(small_hbm, small_operands))
+    ]
     outputs_ref = inputs_ref
     me, sib, cnt, dia = _partners()
     own, depth = inputs_ref.shape
@@ -468,7 +472,7 @@
         )
         for n in range(count)
     ]
-    for load in (*loads[9:], own_tokens, loads[1], own_quarter):
+    for load in (*loads[9:], own_tokens, *small_loads, loads[1], own_quarter):
         load.start()
     small_ref[...] = jnp.zeros_like(small_ref)
     late_ref[...] = jnp.zeros_like(late_ref)
@@ -481,26 +485,31 @@
     for load in (loads[0], loads[3]):
         load.start()
 
-    def project(k, r):
-        place = _rows(blocks[k] * own + r * size, size)
-        part = _nn(tokens_ref[place, :], up_ref[:, : 3 * width])
-        active[place, :width] = (part[:, :width] + qv_bias_ref[:1, :]).astype(bf16)
-        active[place, width : 2 * width] = part[:, width : 2 * width].astype(bf16)
-        active[place, 2 * width : 3 * width] = (part[:, 2 * width :] + qv_bias_ref[1:, :]).astype(bf16)
-        for keep in keeps(k, r):
-            keep.start()
+    def project(ks, r, number):
+        rows = number * size
+        places = [_part(blocks[k] * own + r * size, rows) for k in ks]
+        chunk = jnp.concatenate([tokens_ref[place, :] for place in places], axis=0)
+        for j in range(3):
+            part = _nn(chunk, up_ref[:, j * width : (j + 1) * width])
+            if j != 1:
+                part = part + qv_bias_ref[j // 2 : j // 2 + 1, :]
+            for at, place in enumerate(places):
+                active[place, j * width : (j + 1) * width] = part[at * rows : (at + 1) * rows].astype(bf16)
+        for k in ks:
+            for t in range(number):
+                for keep in keeps(k, r + t):
+                    keep.start()
 
     for load in loads[9:]:
         load.wait()
     own_tokens.wait()
-    loop(lambda r: project(0, r))
+    for load in small_loads:
+        load.wait()
+    out_bias, attn_gain, attn_shift, down_bias, ffn_gain, ffn_shift = [v[...] for v in vector_refs]
+    project([0], 0, CHUNKS)
     full_step(1)
-
-    def sib_part(r):
-        token_copy(r, 0).wait_recv()
-        project(1, r)
-
-    loop(sib_part)
+    loop(lambda r: token_copy(r, 0).wait_recv())
+    project([1], 0, CHUNKS)
     full_step(2)
 
     scaled = _head_masks(heads, width, 1.0 / math.sqrt(HEAD))
@@ -561,9 +570,8 @@
 
         token_copy(r, 1).wait_recv()
         token_copy(r, 2).start()
-        project(2, r)
         token_copy(r, 2).wait_recv()
-        project(3, r)
+        project([2, 3], r, 1)
 
     loop(far_part)
     loads[2].start()
@@ -862,20 +870,34 @@
             query, grad = active[query_rows, :width], back[query_rows, :width]
             rows = _rows(j * BLOCK, BLOCK)
             bias = _bias(seg_ref, pad_ref, query_rows, rows)
-            key, value = active[rows, width : 2 * width], active[rows, 2 * width : 3 * width]
-            key_rows = (key * (1.0 / math.sqrt(HEAD))).astype(bf16).T
-            key_add = jnp.zeros((BLOCK, width), f32)
-            value_add = jnp.zeros((BLOCK, width), f32)
+            queries = [query * scaled[h] for h in range(heads)]
+            context_grads = [grad * plain[h] for h in range(heads)]
+            key_rows = (active[rows, width : 2 * width] * (1.0 / math.sqrt(HEAD))).astype(bf16).T
+            parts = []
+            for c in range(BLOCK // PART):
+                place = pl.ds(pl.multiple_of(j * BLOCK + c * PART, PART), PART)
+                key, value = active[place, width : 2 * width], active[place, 2 * width : 3 * width]
+                probs, score_grads = [], []
+                for h in range(heads):
+                    scores = _nt(key, queries[h]) + bias[c * PART : (c + 1) * PART]
+                    prob = jnp.exp(scores - lse_ref[h : h + 1, query_rows])
+                    probs.append(prob.astype(bf16))
+                    score_grads.append(
+                        (prob * (_nt(value, context_grads[h]) - dots_ref[h : h + 1, :])).astype(bf16)
+                    )
+                spot_rows, spot_cols = spot(j)
+                spot_part = pl.ds(pl.multiple_of(lax.rem(j, per) * BLOCK + c * PART, PART), PART)
+                keys_acc[spot_part, spot_cols] += _nn(
+                    jnp.concatenate(score_grads, axis=1), jnp.concatenate(queries, axis=0)
+                )
+                values_acc[spot_part, spot_cols] += _nn(
+                    jnp.concatenate(probs, axis=1), jnp.concatenate(context_grads, axis=0)
+                )
+                parts.append(score_grads)
             for h in range(heads):
-                query_h, grad_h = query * scaled[h], grad * plain[h]
-                scores = _nt(key, query_h) + bias
-                prob = jnp.exp(scores - lse_ref[h : h + 1, query_rows])
-                score_grad = (prob * (_nt(value, grad_h) - dots_ref[h : h + 1, :])).astype(bf16)
-                key_add = key_add + _nn(score_grad, query_h)
-                value_add = value_add + _nn(prob.astype(bf16), grad_h)
-                query_acc[pl.ds(h * HEAD, HEAD), :] += _nn(key_rows[h * HEAD : (h + 1) * HEAD], score_grad)
-            keys_acc[spot(j)] += key_add
-            values_acc[spot(j)] += value_add
+                query_acc[pl.ds(h * HEAD, HEAD), :] += _nn(
+                    key_rows[h * HEAD : (h + 1) * HEAD], jnp.concatenate([part[h] for part in parts], axis=0)
+                )
 
         @pl.when(turn == 2)
         def _():
@@ -978,7 +1000,7 @@
     return pl.pallas_call(
         partial(main_kernel, bits, pieces),
         out_shape=[jax.ShapeDtypeStruct(*out) for out in outs],
-        in_specs=[REMOTE] * 6 + [LOCAL] * 10,
+        in_specs=[REMOTE] * 16,
         out_specs=[REMOTE] * 7 + [LOCAL],
         scratch_shapes=[
             pltpu.VMEM((whole, width), bf16),
@@ -1016,6 +1038,8 @@
             pltpu.SemaphoreType.DMA((2, 3, CHUNKS)),
             pltpu.SemaphoreType.DMA((2, 4, CHUNKS)),
             pltpu.SemaphoreType.DMA((2, 3 + bits)),
+            pltpu.SemaphoreType.DMA((10,)),
+            *[pltpu.VMEM(array.shape, array.dtype) for array in small_arrays],
         ],
         compiler_params=pltpu.CompilerParams(
             collective_id=1, has_side_effects=True, vmem_limit_bytes=63 * 2**20

time: 276 us -> 272 us (0.986)
  Pallas kernels: 275 us -> 271 us
    pallas_call x1, Pallas kernels: 267 us -> 264 us  [main_layer(): pl.pallas_call(partial(main_kernel, bits, pieces), out_shape=[jax.ShapeDt...]
where the time goes in v1:
time: 272 us
  Pallas kernels  271 us (100%)
    pallas_call x1, Pallas kernels, main_layer(): pl.pallas_call(partial(main_kernel, bits, pieces), out_shape=[jax.ShapeDt...  264 us
    pallas_call x1, Pallas kernels, unpack(): pl.pallas_call(partial(unpack_kernel, width), grid=(steps,), in_specs=[pl...  7.86 us

profile of v1, /device:TPU:0, one launch (start us, length us, event | category | flops | bytes accessed | tf_op | source)
XLA Modules:
  0.0 272.3 jit_solution(14369957903937745066)
XLA Ops:
  0.7 263.6 %main_layer.1 = (bf16[512,1024]{1,0:T(8,128)(2,1)}, bf16[512,1024]{1,0:T(8,128)(2,1)}, bf16[3072,1024]{1,0:T(8,128)(2,1)}, bf16[2048,1024]{1,0:T(8,128)(2,1)}, b...) custom-call(bf16[512,1024]{1,0:T(8,128)(2,1)} %refs_0_.1, ...), custom_call_target="tpu_custom_call" | custom-call | tf_op jit(solution)/shard_map/main_layer/pallas_call | solution.py:1000
  264.2 7.9 %unpack_gradients.1 = (f32[1024,1024]{1,0:T(8,128)}, f32[1024,1024]{1,0:T(8,128)}, f32[3,1024,256]{2,1,0:T(8,128)}, f32[256,1024]{1,0:T(8,128)}, f32[2,256]{1,0:...) custom-call(bf16[3,1024,1024]{2,1,0:T(8,128)(2,1)} %bitcast.15, ...), custom_call_target="tpu_custom_call" | custom-call | tf_op jit(solution)/shard_map/unpack_gradients/pallas_call | solution.py:1089

commit v2 on v1

--- a/solution.py
+++ b/solution.py
@@ -515,12 +515,14 @@
     scaled = _head_masks(heads, width, 1.0 / math.sqrt(HEAD))
     plain = _head_masks(heads, width, 1.0)
 
-    def attention(i):
+    def attention(i, low, high, state=0, begin=True, end=True):
         query_rows = _rows(i * BLOCK, BLOCK)
-        acc = own_acc.at[:width, :BLOCK]
-        peak_ref[...] = jnp.full_like(peak_ref, 2 * NEG)
-        total_ref[...] = jnp.zeros_like(total_ref)
-        acc[...] = jnp.zeros_like(acc)
+        acc = own_acc.at[:width, state * BLOCK : (state + 1) * BLOCK]
+        peaks, totals = [ref.at[state * heads : (state + 1) * heads] for ref in (peak_ref, total_ref)]
+        if begin:
+            peaks[...] = jnp.full_like(peaks, 2 * NEG)
+            totals[...] = jnp.zeros_like(totals)
+            acc[...] = jnp.zeros_like(acc)
 
         def meet(j, carry):
             rows = _rows(j * BLOCK, BLOCK)
@@ -529,23 +531,25 @@
             value = active[rows, 2 * width : 3 * width].T
             for h in range(heads):
                 scores = _nt(key, query * scaled[h]) + bias
-                old = peak_ref[h]
+                old = peaks[h]
                 peak = jnp.maximum(old, jnp.max(scores, axis=0, keepdims=True))
                 expo = jnp.exp(scores - peak)
                 ratio = jnp.exp(old - peak)
-                peak_ref[h] = peak
-                total_ref[h] = total_ref[h] * ratio + jnp.sum(expo, axis=0, keepdims=True)
+                peaks[h] = peak
+                totals[h] = totals[h] * ratio + jnp.sum(expo, axis=0, keepdims=True)
                 place = pl.ds(h * HEAD, HEAD)
                 acc[place, :] = acc[place, :] * ratio + _nn(
                     value[h * HEAD : (h + 1) * HEAD], expo.astype(bf16)
                 )
             return carry
 
-        lax.fori_loop(jnp.maximum(i - 1, 0), jnp.minimum(i + 2, token_blocks), meet, 0)
+        lax.fori_loop(low, high, meet, 0)
+        if not end:
+            return
         for h in range(heads):
             place = pl.ds(h * HEAD, HEAD)
-            acc[place, :] = acc[place, :] / total_ref[h]
-            lse_ref[h : h + 1, query_rows] = peak_ref[h] + jnp.log(total_ref[h])
+            acc[place, :] = acc[place, :] / totals[h]
+            lse_ref[h : h + 1, query_rows] = peaks[h] + jnp.log(totals[h])
         back[query_rows, :width] = acc[...].astype(bf16).T
 
     half = token_blocks // 2
@@ -554,9 +558,14 @@
     chunks_per = BLOCK // size
 
     def near(p):
-        attention(jnp.where(chip == 0, p, token_blocks - 1 - p))
+        around(jnp.where(chip == 0, p, token_blocks - 1 - p))
+
+    def around(i):
+        attention(i, jnp.maximum(i - 1, 0), jnp.minimum(i + 2, token_blocks))
 
     _loop(half - 1, near)
+    edge = half - 1 + chip
+    attention(edge, half - 2 + 2 * chip, half + 2 * chip, 1, end=False)
 
     def far_part(r):
         @pl.when(r == 0)
@@ -588,7 +597,7 @@
 
     def far(p):
         k, h = lax.rem(p, 2), p // 2
-        attention(jnp.where(k == 0, cnt, dia) * per_device + h)
+        around(jnp.where(k == 0, cnt, dia) * per_device + h)
 
         @pl.when(p == 0)
         def _():
@@ -602,7 +611,7 @@
                     trade(h * chunks_per + t, 2 + c).start()
 
     _loop(2 * per_device, far)
-    attention(jnp.where(chip == 0, half - 1, half))
+    attention(edge, half - chip, half - chip + 1, 1, begin=False)
     loop(lambda r: trade(r, 1).start())
     own_context.start()
     save_context = pltpu.make_async_copy(back.at[:, :width], context_hbm, load_sems.at[15])
@@ -1016,8 +1025,8 @@
             pltpu.VMEM((own, depth), f32),
             pltpu.VMEM((8, BLOCK), f32),
             pltpu.VMEM((8, whole), f32),
-            pltpu.VMEM((width // HEAD, 1, BLOCK), f32),
-            pltpu.VMEM((width // HEAD, 1, BLOCK), f32),
+            pltpu.VMEM((2 * (width // HEAD), 1, BLOCK), f32),
+            pltpu.VMEM((2 * (width // HEAD), 1, BLOCK), f32),
             *_scatter_scratch(own, depth),
             pltpu.VMEM((3 * pieces * (depth // pieces - (depth // pieces >> bits)), depth), bf16),
             pltpu.VMEM((3 * depth, depth), bf16),

time: 272 us -> 272 us (level)
  no operation moved by 1% of the time
where the time goes in v2:
time: 272 us
  Pallas kernels  271 us (100%)
    pallas_call x1, Pallas kernels, main_layer(): pl.pallas_call(partial(main_kernel, bits, pieces), out_shape=[jax.ShapeDt...  263 us
    pallas_call x1, Pallas kernels, unpack(): pl.pallas_call(partial(unpack_kernel, width), grid=(steps,), in_specs=[pl...  7.86 us

profile of v2, /device:TPU:0, one launch (start us, length us, event | category | flops | bytes accessed | tf_op | source)
XLA Modules:
  0.0 271.8 jit_solution(5089809132072771312)
XLA Ops:
  0.7 263.1 %main_layer.1 = (bf16[512,1024]{1,0:T(8,128)(2,1)}, bf16[512,1024]{1,0:T(8,128)(2,1)}, bf16[3072,1024]{1,0:T(8,128)(2,1)}, bf16[2048,1024]{1,0:T(8,128)(2,1)}, b...) custom-call(bf16[512,1024]{1,0:T(8,128)(2,1)} %refs_0_.1, ...), custom_call_target="tpu_custom_call" | custom-call | tf_op jit(solution)/shard_map/main_layer/pallas_call | solution.py:1009
  263.7 7.9 %unpack_gradients.1 = (f32[1024,1024]{1,0:T(8,128)}, f32[1024,1024]{1,0:T(8,128)}, f32[3,1024,256]{2,1,0:T(8,128)}, f32[256,1024]{1,0:T(8,128)}, f32[2,256]{1,0:...) custom-call(bf16[3,1024,1024]{2,1,0:T(8,128)(2,1)} %bitcast.15, ...), custom_call_target="tpu_custom_call" | custom-call | tf_op jit(solution)/shard_map/unpack_gradients/pallas_call | solution.py:1098
